TPU v7x, 32 devices: a whole 2x2x4 slice. The times are simulated.
32 devices in a mesh: clip: 8 (over z, x), grp: 4 (over y, core).
Axes of the slice: x: 2, y: 2, z: 4, core: 2. Of those that a mesh axis runs over, the one named last changes fastest.
Arguments:
- hidden: bfloat16 [8, 20, 256, 1152], P('clip', 'grp'), may hold values from -6 to 6
- modulation: float32 [8, 3, 1152], P('clip'), may hold values from -3 to 3
- clip_frames: int32 [8], P('clip'), may hold values from 1 to 20, as said below
- qkv_weight: bfloat16 [1152, 3456], P(None, ('clip', 'grp')), may hold values from -0.1875 to 0.1875
- out_weight: bfloat16 [1152, 1152], P(None, ('clip', 'grp')), may hold values from -0.1875 to 0.1875
Outputs:
- output: bfloat16 [8, 20, 256, 1152], P('clip', 'grp')
Inputs may be any that keep to these rules, and one draw needn't show every extreme that they name: `clip_frames`: at least one clip has all 20 frames.
All inputs are finite; a program needn't handle non-finite values.
Results may differ from a plain program's by a relative error of at most 0.0085.
Values may be sent and summed in bfloat16 or wider, within the bound.
A program may use at most 128 MiB of HBM per device.

v0:
```python
import jax
import jax.numpy as jnp
from jax import lax
from jax.sharding import PartitionSpec as P

HEADS = 16


def modulate(features, table):
    average = jnp.mean(features, axis=-1, keepdims=True)
    centred = features - average
    variance = jnp.mean(centred * centred, axis=-1, keepdims=True)
    normed = centred * lax.rsqrt(variance + 1e-06)
    return (normed * (1.0 + table[1]) + table[0]).astype(jnp.bfloat16)


def on_device(hidden, modulation, clip_frames, qkv_weight, out_weight):
    own_frames = hidden.shape[1]
    frame_tokens = hidden.shape[2]
    model_width = hidden.shape[3]
    group_size = lax.axis_size("grp")
    total_frames = own_frames * group_size
    cell_count = frame_tokens // group_size
    head_count = HEADS
    head_width = model_width // head_count
    table = modulation[0]
    length = clip_frames[0]
    features = hidden[0].astype(jnp.float32)
    modulated = modulate(features, table)
    frame_rows = modulated.reshape(own_frames * frame_tokens, model_width)
    qkv_rows = jnp.dot(
        frame_rows,
        lax.all_gather(qkv_weight, ("clip", "grp"), axis=1, tiled=True),
        preferred_element_type=jnp.float32,
    ).astype(jnp.bfloat16)
    qkv_rows = qkv_rows.reshape(own_frames, frame_tokens, 3 * model_width)
    qkv_rows = lax.all_to_all(qkv_rows, "grp", split_axis=1, concat_axis=0, tiled=True)
    query_heads = qkv_rows[:, :, :model_width].reshape(
        total_frames, cell_count, head_count, head_width
    )
    key_heads = qkv_rows[:, :, model_width : 2 * model_width].reshape(
        total_frames, cell_count, head_count, head_width
    )
    value_heads = qkv_rows[:, :, 2 * model_width :].reshape(
        total_frames, cell_count, head_count, head_width
    )
    scores = jnp.einsum(
        "fshd,gshd->hfgs", query_heads, key_heads, preferred_element_type=jnp.float32
    ) * head_width ** (-0.5)
    key_live = jnp.arange(total_frames) < length
    scores = jnp.where(key_live[None, None, :, None], scores, -1e30)
    attn_weights = jax.nn.softmax(scores, axis=2).astype(jnp.bfloat16)
    mixed = jnp.einsum(
        "hfgs,gshd->fshd", attn_weights, value_heads, preferred_element_type=jnp.float32
    ).astype(jnp.bfloat16)
    mixed = mixed.reshape(total_frames, cell_count, model_width)
    returned = lax.all_to_all(mixed, "grp", split_axis=0, concat_axis=1, tiled=True)
    attn_rows = returned.reshape(own_frames * frame_tokens, model_width)
    first_frame = lax.axis_index("grp") * own_frames
    frame_live = (first_frame + jnp.arange(own_frames) < length).astype(jnp.float32)
    gate_row = table[2]
    block_cols = lax.all_gather(out_weight, ("clip", "grp"), axis=1, tiled=True)
    col_count = block_cols.shape[1]
    projected = jnp.dot(attn_rows, block_cols, preferred_element_type=jnp.float32).reshape(
        own_frames, frame_tokens, col_count
    )
    result = (features + gate_row * projected * frame_live[:, None, None]).astype(jnp.bfloat16)
    return result[None]


def solution(mesh):
    placed = (
        P("clip", "grp", None, None),
        P("clip", None, None),
        P("clip"),
        P(None, ("clip", "grp")),
        P(None, ("clip", "grp")),
    )
    return jax.shard_map(
        on_device,
        mesh=mesh,
        in_specs=placed,
        out_specs=P("clip", "grp", None, None),
        check_vma=False,
    )
```

profile of v0, /device:TPU:17, one launch (start us, length us, event | category | flops | bytes accessed | tf_op | source)
XLA Modules:
  0.0 462.8 jit_solution(12851494021922097695)
XLA Ops:
  6.5 0.0 copy-start
  6.5 0.0 copy-start.2
  6.5 0.0 all-gather.5.cloned.1.call-start
  6.5 0.7 all-gather.5.cloned.1.call-update
  7.3 2.4 convert_reduce_fusion
  9.7 2.8 fusion.19
  12.5 0.0 copy-done.2
  12.5 0.0 copy-done
  12.5 2.7 fusion.17
  15.3 72.8 %all-gather.5.cloned.1.call-done = bf16[32,108,1152]{2,1,0:T(8,128)(2,1)} async-done(((bf16[1,108,1152]{2,1,0:T(8,128)(2,1)}), bf16[32,108,1152]{2,1,0:T(8,128)(2,1)}) %all-gather.5.cloned.1.call-update) | async-done | bytes 7962640 | tf_op jit(solution)/shard_map/all_gather | solution.py:33
  88.1 9.2 %reshape.75 = bf16[3456,1152]{1,0:T(8,128)(2,1)} reshape(bf16[32,108,1152]{2,1,0:T(8,128)(2,1)} %all-gather.5.cloned.1.call-done) | data formatting | bytes 15925248
  97.3 18.0 %convolution_convert_fusion = bf16[1280,3456]{1,0:T(8,128)(2,1)} fusion(bf16[1280,1152]{1,0:T(8,128)(2,1)} %fusion.17, bf16[3456,1152]{1,0:T(8,128)(2,1)} %reshape.75), kind=kOutput, calls=%fused_computation.1 | convolution fusion | flops 10196582400 | bytes 19759104 | tf_op jit(solution)/shard_map/dot_general | solution.py:31
  115.3 13.5 %copy.20 = bf16[5,256,3456]{2,0,1:T(8,128)(2,1)} copy(bf16[5,256,3456]{2,1,0:T(8,128)(2,1)} %bitcast.61) | data formatting | bytes 17694720 | tf_op jit(solution)/shard_map/reshape | solution.py:36
  128.8 6.7 %all-to-all-start = ((bf16[5,256,3456]{2,0,1:T(8,128)(2,1)}), bf16[5,256,3456]{2,0,1:T(8,128)(2,1)}, u32[]{:S(2)}, u32[]{:S(2)}) async-start(bf16[5,256,3456]{2,0,1:T(8,128)(2,1)} %copy.20), calls=%async_computation | async-start | bytes 28311552 | tf_op jit(solution)/shard_map/all_to_all | solution.py:37
  135.5 0.3 all-gather.7.cloned.1.call-start
  135.8 0.5 all-gather.7.cloned.1.call-update
  136.9 160.0 %all-to-all-done = bf16[5,256,3456]{2,0,1:T(8,128)(2,1)} async-done(((bf16[5,256,3456]{2,0,1:T(8,128)(2,1)}), bf16[5,256,3456]{2,0,1:T(8,128)(2,1)}, u32[]{:S(2)}, u32[]{:S(2)}) %all-to-all-start) | async-done | bytes 8847392 | tf_op jit(solution)/shard_map/all_to_all | solution.py:37
  296.9 6.9 %copy.22 = bf16[4,5,64,3456]{3,2,1,0:T(8,128)(2,1)S(1)} copy(bf16[4,5,64,3456]{3,1,2,0:T(8,128)(2,1)} %bitcast.7) | data formatting | bytes 17694720 | tf_op jit(solution)/shard_map/all_to_all | solution.py:37
  303.8 3.6 fusion.28
  307.5 11.6 %reshape.70 = bf16[20,64,16,72]{3,2,1,0:T(8,128)(2,1)} reshape(bf16[20,64,1152]{2,1,0:T(8,128)(2,1)} %get-tuple-element.10) | data formatting | bytes 5898240 | tf_op jit(solution)/shard_map/reshape | solution.py:41
  319.1 11.6 %reshape.71 = bf16[20,64,16,72]{3,2,1,0:T(8,128)(2,1)} reshape(bf16[20,64,1152]{2,1,0:T(8,128)(2,1)} %get-tuple-element.9) | data formatting | bytes 5898240 | tf_op jit(solution)/shard_map/reshape | solution.py:38
  330.7 11.6 %reshape.69 = bf16[20,64,16,72]{3,2,1,0:T(8,128)(2,1)} reshape(bf16[20,64,1152]{2,1,0:T(8,128)(2,1)} %get-tuple-element.8) | data formatting | bytes 5898240 | tf_op jit(solution)/shard_map/reshape | solution.py:44
  342.3 28.1 %fusion.8 = f32[16,64,20,20]{3,2,1,0:T(8,128)} fusion(bf16[20,64,16,72]{3,2,1,0:T(8,128)(2,1)} %reshape.71, bf16[20,64,16,72]{3,2,1,0:T(8,128)(2,1)} %reshape.70), kind=kOutput, calls=%fused_computation.11 | convolution fusion | flops 58982400 | bytes 7536640 | tf_op jit(solution)/shard_map/fshd,gshd->hfgs/dot_general | solution.py:47
  370.4 16.4 %fusion.29 = (f32[16,20,64]{1,2,0:T(8,128)S(1)}, f32[16,20,20,64]{1,2,3,0:T(8,128)}) fusion(f32[16,64,20,20]{3,2,1,0:T(8,128)} %fusion.8, pred[20]{0:T(512)(128)(4,1)S(1)} %iota_compare_fusion), kind=kOutput, calls=%fused_computation.40 | output fusion | flops 2457619 | bytes 3358740 | tf_op jit(solution)/shard_map/sub | solution.py:52
  386.8 8.6 %convert_bitcast_fusion = bf16[20,64,16,72]{3,0,2,1:T(8,128)(2,1)S(1)} fusion(bf16[20,64,16,72]{3,2,1,0:T(8,128)(2,1)} %reshape.69, f32[16,20,20,64]{1,2,3,0:T(8,128)} %get-tuple-element.12, f32[16,20,64]{1,2,0:T(8,128)S(1)} %get-tuple-element.11), kind=kOutput, calls=%fused_computation.14 | convolution fusion | flops 61276160 | bytes 7618560 | tf_op jit(solution)/shard_map/hfgs,gshd->fshd/dot_general | solution.py:53
  395.4 3.4 copy.27
  398.8 9.0 %reshape.72 = bf16[20,64,1152]{2,1,0:T(8,128)(2,1)} reshape(bf16[20,64,16,72]{3,2,1,0:T(8,128)(2,1)} %copy.27) | data formatting | bytes 5898240 | tf_op jit(solution)/shard_map/reshape | solution.py:56
  407.9 5.4 %all-to-all-start.1 = ((bf16[20,64,1152]{2,1,0:T(8,128)(2,1)}), bf16[20,64,1152]{2,1,0:T(8,128)(2,1)}, u32[]{:S(2)}, u32[]{:S(2)}) async-start(bf16[20,64,1152]{2,1,0:T(8,128)(2,1)} %reshape.72), calls=%async_computation.1 | async-start | bytes 5898240 | tf_op jit(solution)/shard_map/all_to_all | solution.py:57
  413.3 0.0 all-gather.7.cloned.1.call-done
  413.3 5.1 %reshape.78 = bf16[1152,1152,1]{1,0,2:T(8,128)(2,1)} reshape(bf16[32,36,1152]{2,1,0:T(8,128)(2,1)} %all-gather.7.cloned.1.call-done) | data formatting | bytes 5308416
  418.4 28.9 %all-to-all-done.1 = bf16[20,64,1152]{2,1,0:T(8,128)(2,1)} async-done(((bf16[20,64,1152]{2,1,0:T(8,128)(2,1)}), bf16[20,64,1152]{2,1,0:T(8,128)(2,1)}, u32[]{:S(2)}, u32[]{:S(2)}) %all-to-all-start.1) | async-done | bytes 2949152 | tf_op jit(solution)/shard_map/all_to_all | solution.py:57
  447.4 0.0 copy-start.1
  447.4 2.2 copy.28
  449.6 0.4 copy-done.1
  450.0 5.8 %fusion.21 = bf16[1,5,256,1152]{3,2,1,0:T(8,128)(2,1)} fusion(bf16[5,256,1152]{2,1,0:T(8,128)(2,1)S(1)} %bitcast.62, bf16[1152,1152,1]{1,0,2:T(8,128)(2,1)S(1)} %copy-done.1, bf16[1,5,256,1152]{3,2,1,0:T(8,128)(2,1)S(1)} %copy-done, f32[5]{0:T(128)S(1)} %compare_convert_fusion, f32[1152]{0:T(1024)S(1)} %get-tuple-element.5), kind=kOutput, calls=%fused_computation.29 | convolution fusion | flops 3404759040 | bytes 11506196 | tf_op jit(solution)/shard_map/dot_general | solution.py:64
  (7 shorter events, 0.1 us)
Async XLA Ops:
  6.5 6.0 %copy-start = (bf16[1,5,256,1152]{3,2,1,0:T(8,128)(2,1)S(1)}, bf16[1,5,256,1152]{3,2,1,0:T(8,128)(2,1)}, u32[]{:S(2)}) copy-start(bf16[1,5,256,1152]{3,2,1,0:T(8,128)(2,1)} %param.5) | copy-start | bytes 8847364
  6.5 5.9 %copy-start.2 = (f32[1,3,1152]{2,0,1:T(1,128)S(1)}, f32[1,3,1152]{2,0,1:T(1,128)}, u32[]{:S(2)}) copy-start(f32[1,3,1152]{2,0,1:T(1,128)} %param.6) | copy-start | bytes 41476
  6.5 81.5 %all-gather.5.cloned.1.call-start = ((), (), s32[]{:S(2)}) async-start(), calls=%async_computation.2 | async-start | bytes 8515584 | tf_op jit(solution)/shard_map/all_gather | solution.py:33
  128.8 168.1 %all-to-all-start = ((bf16[5,256,3456]{2,0,1:T(8,128)(2,1)}), bf16[5,256,3456]{2,0,1:T(8,128)(2,1)}, u32[]{:S(2)}, u32[]{:S(2)}) async-start(bf16[5,256,3456]{2,0,1:T(8,128)(2,1)} %copy.20), calls=%async_computation | async-start | bytes 28311552 | tf_op jit(solution)/shard_map/all_to_all | solution.py:37
  135.5 277.8 %all-gather.7.cloned.1.call-start = ((), (), s32[]{:S(2)}) async-start(), calls=%async_computation.3 | async-start | bytes 3041280 | tf_op jit(solution)/shard_map/all_gather | solution.py:62
  407.9 39.5 %all-to-all-start.1 = ((bf16[20,64,1152]{2,1,0:T(8,128)(2,1)}), bf16[20,64,1152]{2,1,0:T(8,128)(2,1)}, u32[]{:S(2)}, u32[]{:S(2)}) async-start(bf16[20,64,1152]{2,1,0:T(8,128)(2,1)} %reshape.72), calls=%async_computation.1 | async-start | bytes 5898240 | tf_op jit(solution)/shard_map/all_to_all | solution.py:57
  447.4 2.6 copy-start.1
Sparse Core Ops, SparseCore 0:
  10.3 77.7 all-gather.4
  139.2 62.9 all-gather.6
where the time goes:
time: 469 us; the launch traced here: 463 us
  waiting for transfers between devices  263 us (56%)
  local copies, waits for them, and re-layouts  88.4 us (19%)
  matrix products  60.4 us (13%)
  other arithmetic  24.4 us (5%)
  between operations  14.3 us (3%)
  starting transfers between devices  12.4 us (3%)
    all_to_all x1, waiting for transfers between devices, on_device(): lax.all_to_all(qkv_rows, 'grp', split_axis=1, concat_axis=0, tiled=True)  160 us
    all_gather x1, waiting for transfers between devices, on_device(): lax.all_gather(qkv_weight, ('clip', 'grp'), axis=1, tiled=True)  72.8 us
    all_to_all x1, waiting for transfers between devices, on_device(): lax.all_to_all(mixed, 'grp', split_axis=0, concat_axis=1, tiled=True)  28.9 us
    dot_general x1, matrix products, on_device(): jnp.einsum('fshd,gshd->hfgs', query_heads, key_heads, preferred_element_t...  28.1 us
    dot_general x1, matrix products, on_device(): jnp.dot(frame_rows, lax.all_gather(qkv_weight, ('clip', 'grp'), axis=1, t...  18 us
    sub x1, other arithmetic, on_device(): attn_weights = jax.nn.softmax(scores, axis=2).astype(jnp.bfloat16)  16.4 us
    unnamed x8, local copies, waits for them, and re-layouts  14.8 us
    reshape x1, local copies, waits for them, and re-layouts, on_device(): qkv_rows = qkv_rows.reshape(own_frames, frame_tokens, 3 * model_width)  13.5 us
  transfers between devices with their start and end apart: 4, of which 3 were waited for; matrix products, arithmetic and copies ran while one was open for 27% of the time, Pallas kernels for 0%

commit v1 on v0

v1 whole, which is shorter than its diff:
```python
import functools

import jax
import jax.numpy as jnp
from jax import lax
from jax.experimental import pallas as pl
from jax.experimental.pallas import tpu as pltpu
from jax.sharding import PartitionSpec as P

HEADS = 16
HALF = 8
PAIR = 16
LOG2E = 1.4426950408889634
NT = (((1,), (1,)), ((), ()))


def col_tile(cols):
    return 384 if cols % 384 == 0 else 128


def make_bias(bias_ref, length):
    keys = bias_ref.shape[1]
    row = lax.broadcasted_iota(jnp.int32, bias_ref.shape, 0)
    col = lax.broadcasted_iota(jnp.int32, bias_ref.shape, 1)
    same = (row % HALF) == (col % HALF)
    live = (col // HALF) < length
    bias_ref[...] = jnp.where(same & live, 0.0, -1e30).astype(jnp.float32)


def modulate_step(step, x_ref, table_ref, mod_ref):
    frames, tokens, width = x_ref.shape
    pairs = frames // 2
    block = step // pairs
    pair = step % pairs
    x = x_ref[pl.ds(2 * pair, 2), pl.ds(PAIR * block, PAIR), :].astype(jnp.float32)
    mean = jnp.sum(x, axis=-1, keepdims=True) * (1.0 / width)
    centred = x - mean
    var = jnp.sum(centred * centred, axis=-1, keepdims=True) * (1.0 / width)
    normed = centred * lax.rsqrt(var + 1e-06)
    y = normed * (1.0 + table_ref[1:2, :])[None] + table_ref[0:1, :][None]
    for half in range(2):
        part = y[:, half * HALF : (half + 1) * HALF, :].reshape(2 * HALF, width)
        start = pl.multiple_of((2 * block + half) * frames * HALF + pair * 2 * HALF, 16)
        mod_ref[pl.ds(start, 2 * HALF), :] = part.astype(jnp.bfloat16)


def qkv_step(step, mod_ref, wqkv_ref, qkv_ref, rows, first=0):
    count = mod_ref.shape[0] // rows
    tile = col_tile(wqkv_ref.shape[0])
    n = pl.multiple_of((first + step // count) * tile, 128)
    m = pl.multiple_of((step % count) * rows, 16)
    got = lax.dot_general(
        mod_ref[pl.ds(m, rows), :], wqkv_ref[pl.ds(n, tile), :], NT,
        preferred_element_type=jnp.float32,
    )
    qkv_ref[pl.ds(m, rows), pl.ds(n, tile)] = got.astype(jnp.bfloat16)


def attend(start, rows, width, qkv_ref, bias_ref, mixed_ref, mixed_start):
    head = width // HEADS
    scale = head**-0.5 * LOG2E
    tiles = [None] * (width // 128)
    for h in range(HEADS):
        low, high = h * head, (h + 1) * head
        w0 = low // 128 * 128
        w1 = (high + 127) // 128 * 128
        lane = lax.broadcasted_iota(jnp.int32, (1, w1 - w0), 1) + w0
        inside = (lane >= low) & (lane < high)
        q = qkv_ref[pl.ds(start, rows), w0:w1]
        k = qkv_ref[pl.ds(start, rows), width + w0 : width + w1]
        v = qkv_ref[pl.ds(start, rows), 2 * width + w0 : 2 * width + w1]
        q = q * jnp.where(inside, 1.0, 0.0).astype(jnp.bfloat16)
        s = lax.dot_general(q, k, NT, preferred_element_type=jnp.float32)
        s = s * scale + bias_ref[...]
        p = jnp.exp2(s - jnp.max(s, axis=-1, keepdims=True))
        total = jnp.sum(p, axis=-1, keepdims=True)
        o = jnp.dot(p.astype(jnp.bfloat16), v, preferred_element_type=jnp.float32)
        o = o * (1.0 / total)
        for t in range(w0 // 128, w1 // 128):
            part = o[:, t * 128 - w0 : t * 128 - w0 + 128]
            where = inside[:, t * 128 - w0 : t * 128 - w0 + 128]
            tiles[t] = part if tiles[t] is None else jnp.where(where, part, tiles[t])
            if high >= (t + 1) * 128:
                mixed_ref[pl.ds(mixed_start, rows), t * 128 : (t + 1) * 128] = tiles[t].astype(
                    jnp.bfloat16
                )


def finish_block(block, x_ref, table_ref, length, qkv_ref, bias_ref, mixed_ref, proj_ref, wout_ref, out_ref):
    frames, tokens, width = x_ref.shape
    rows = frames * HALF

    def half_step(half, carry):
        start = pl.multiple_of((2 * block + half) * rows, 16)
        attend(start, rows, width, qkv_ref, bias_ref, mixed_ref, pl.multiple_of(half * rows, 16))
        return carry

    lax.fori_loop(0, 2, half_step, 0)
    tile = col_tile(width)
    def project(n, carry):
        at = pl.multiple_of(n * tile, 128)
        proj_ref[:, pl.ds(at, tile)] = lax.dot_general(
            mixed_ref[...], wout_ref[pl.ds(at, tile), :], NT, preferred_element_type=jnp.float32
        )
        return carry

    lax.fori_loop(0, width // tile, project, 0)
    gate = table_ref[2:3, :]

    def close(f, carry):
        at = pl.multiple_of(f * HALF, HALF)
        top = proj_ref[pl.ds(at, HALF), :]
        low = proj_ref[pl.ds(pl.multiple_of(rows + at, HALF), HALF), :]
        got = jnp.concatenate([top, low], axis=0)
        live = jnp.where(f < length, 1.0, 0.0).astype(jnp.float32)
        x = x_ref[f, pl.ds(pl.multiple_of(PAIR * block, PAIR), PAIR), :].astype(jnp.float32)
        out_ref[f, pl.ds(pl.multiple_of(PAIR * block, PAIR), PAIR), :] = (
            x + gate * got * live
        ).astype(jnp.bfloat16)
        return carry

    lax.fori_loop(0, frames, close, 0)


def kernel(len_ref, x_ref, table_ref, wqkv_ref, wout_ref, out_ref, mod_ref, qkv_ref, bias_ref, mixed_ref, proj_ref):
    frames, tokens, width = x_ref.shape
    length = len_ref[0]
    make_bias(bias_ref, length)

    def first(step, carry):
        modulate_step(step, x_ref, table_ref, mod_ref)
        return carry

    lax.fori_loop(0, frames // 2 * (tokens // PAIR), first, 0)
    rows = 2 * frames * HALF

    def second(step, carry):
        qkv_step(step, mod_ref, wqkv_ref, qkv_ref, rows)
        return carry

    lax.fori_loop(0, (mod_ref.shape[0] // rows) * (3 * width // col_tile(3 * width)), second, 0)

    def third(block, carry):
        finish_block(block, x_ref, table_ref, length, qkv_ref, bias_ref, mixed_ref, proj_ref, wout_ref, out_ref)
        return carry

    lax.fori_loop(0, tokens // PAIR, third, 0)


def on_device(hidden, modulation, clip_frames, qkv_weight, out_weight):
    both = ("clip", "grp")
    wqkv = lax.all_gather(qkv_weight.T, both, axis=0, tiled=True)
    wout = lax.all_gather(out_weight.T, both, axis=0, tiled=True)
    x = lax.all_to_all(hidden[0], "grp", split_axis=1, concat_axis=0, tiled=True)
    frames, tokens, width = x.shape
    rows = frames * HALF
    vmem = pl.BlockSpec(memory_space=pltpu.VMEM)
    out = pl.pallas_call(
        kernel,
        out_shape=jax.ShapeDtypeStruct(x.shape, jnp.bfloat16),
        in_specs=[pl.BlockSpec(memory_space=pltpu.SMEM)] + [vmem] * 4,
        out_specs=vmem,
        scratch_shapes=[
            pltpu.VMEM((frames * tokens, width), jnp.bfloat16),
            pltpu.VMEM((frames * tokens, 3 * width), jnp.bfloat16),
            pltpu.VMEM((rows, rows), jnp.float32),
            pltpu.VMEM((2 * rows, width), jnp.bfloat16),
            pltpu.VMEM((2 * rows, width), jnp.float32),
        ],
        compiler_params=pltpu.CompilerParams(vmem_limit_bytes=56 * 1024 * 1024),
    )(clip_frames, x, modulation[0], wqkv, wout)
    return lax.all_to_all(out, "grp", split_axis=0, concat_axis=1, tiled=True)[None]


def solution(mesh):
    placed = (
        P("clip", "grp", None, None),
        P("clip", None, None),
        P("clip"),
        P(None, ("clip", "grp")),
        P(None, ("clip", "grp")),
    )
    return jax.shard_map(
        on_device,
        mesh=mesh,
        in_specs=placed,
        out_specs=P("clip", "grp", None, None),
        check_vma=False,
    )
```

time: 469 us -> 267 us (0.57)
  waiting for transfers between devices: 263 us -> 124 us
  local copies, waits for them, and re-layouts: 88.4 us -> 27.1 us
  matrix products: 60.4 us -> 0 us
  Pallas kernels: 0 us -> 55.5 us
  blocking collectives: 0 us -> 38 us
  other arithmetic: 24.4 us -> 0 us
  starting transfers between devices: 12.4 us -> 5.74 us
    all_to_all x2 -> x1, waiting for transfers between devices: 189 us -> 59.1 us  [on_device(): lax.all_to_all(hidden[0], 'grp', split_axis=1, concat_axis=0, tiled=True)]
    dot_general x4 -> x0, matrix products: 60.4 us -> none  [the longest x1 28.1 us: on_device(): jnp.einsum('fshd,gshd->hfgs', query_heads, key_heads, preferred_element_t...]
    reshape x5 -> x0, local copies, waits for them, and re-layouts: 57.4 us -> none  [the longest x1 13.5 us: on_device(): qkv_rows = qkv_rows.reshape(own_frames, frame_tokens, 3 * model_width)]
    pallas_call x0 -> x1, Pallas kernels: none -> 55.5 us  [on_device(): pl.pallas_call(kernel, out_shape=jax.ShapeDtypeStruct(x.shape, jnp.bfloat...]
    all_to_all x0 -> x1, blocking collectives: none -> 38 us  [on_device(): lax.all_to_all(out, 'grp', split_axis=0, concat_axis=1, tiled=True)[None]]
    sub x1 -> x0, other arithmetic: 16.4 us -> none  [on_device(): attn_weights = jax.nn.softmax(scores, axis=2).astype(jnp.bfloat16)]
    all_gather x2, waiting for transfers between devices: 72.8 us -> 63.2 us  [the longest x1 63.2 us: on_device(): wqkv = lax.all_gather(qkv_weight.T, both, axis=0, tiled=True)]
    all_to_all x2 -> x1, starting transfers between devices: 12.2 us -> 5.7 us  [on_device(): lax.all_to_all(hidden[0], 'grp', split_axis=1, concat_axis=0, tiled=True)]
  transfers between devices with their start and end apart: 4 -> 3, of which waited for: 3 -> 2; matrix products, arithmetic and copies ran while one was open for 27% -> 6% of each run, Pallas kernels for 0% -> 0%
where the time goes in v1:
time: 267 us; the launch traced here: 264 us
  waiting for transfers between devices  124 us (46%)
  Pallas kernels  55.5 us (21%)
  blocking collectives  38 us (14%)
  local copies, waits for them, and re-layouts  27.1 us (10%)
  between operations  14.1 us (5%)
  starting transfers between devices  5.74 us (2%)
    all_gather x1, waiting for transfers between devices, on_device(): wqkv = lax.all_gather(qkv_weight.T, both, axis=0, tiled=True)  63.2 us
    all_to_all x1, waiting for transfers between devices, on_device(): lax.all_to_all(hidden[0], 'grp', split_axis=1, concat_axis=0, tiled=True)  59.1 us
    pallas_call x1, Pallas kernels, on_device(): pl.pallas_call(kernel, out_shape=jax.ShapeDtypeStruct(x.shape, jnp.bfloat...  55.5 us
    all_to_all x1, blocking collectives, on_device(): lax.all_to_all(out, 'grp', split_axis=0, concat_axis=1, tiled=True)[None]  38 us
    unnamed x6, local copies, waits for them, and re-layouts  20.8 us
    all_to_all x1, starting transfers between devices, on_device(): lax.all_to_all(hidden[0], 'grp', split_axis=1, concat_axis=0, tiled=True)  5.7 us
  transfers between devices with their start and end apart: 3, of which 2 were waited for; matrix products, arithmetic and copies ran while one was open for 6% of the time, Pallas kernels for 0%

profile of v1, /device:TPU:17, one launch (start us, length us, event | category | flops | bytes accessed | tf_op | source)
XLA Modules:
  0.0 264.1 jit_solution(14912498623161202223)
XLA Ops:
  6.5 0.0 all-gather.7.cloned.1.call-start
  6.5 0.7 all-gather.7.cloned.1.call-update
  7.3 0.0 all-gather.5.cloned.1.call-start
  7.3 0.7 all-gather.5.cloned.1.call-update
  8.0 5.8 %copy.16 = bf16[1,5,256,1152]{3,1,2,0:T(8,128)(2,1)} copy(bf16[1,5,256,1152]{3,2,1,0:T(8,128)(2,1)} %param.5) | data formatting | bytes 5898240 | tf_op args[0]
  13.8 0.0 copy-start
  13.8 5.7 %all-to-all-start = ((bf16[5,256,1152]{2,0,1:T(8,128)(2,1)}), bf16[5,256,1152]{2,0,1:T(8,128)(2,1)}, u32[]{:S(2)}, u32[]{:S(2)}) async-start(bf16[5,256,1152]{2,0,1:T(8,128)(2,1)} %bitcast.20), calls=%async_computation | async-start | bytes 9437184 | tf_op jit(solution)/shard_map/all_to_all | solution.py:154
  19.5 0.0 copy-done
  19.5 0.6 copy.17
  20.7 59.1 %all-to-all-done = bf16[5,256,1152]{2,0,1:T(8,128)(2,1)} async-done(((bf16[5,256,1152]{2,0,1:T(8,128)(2,1)}), bf16[5,256,1152]{2,0,1:T(8,128)(2,1)}, u32[]{:S(2)}, u32[]{:S(2)}) %all-to-all-start) | async-done | bytes 2949152 | tf_op jit(solution)/shard_map/all_to_all | solution.py:154
  79.8 4.5 %copy.11 = bf16[5,4,64,1152]{3,2,0,1:T(8,128)(2,1)} copy(bf16[5,4,64,1152]{3,0,2,1:T(8,128)(2,1)} %bitcast.1) | data formatting | bytes 5898240 | tf_op jit(solution)/shard_map/all_to_all | solution.py:154
  84.3 0.0 all-gather.7.cloned.1.call-done
  84.3 5.2 %reshape.4.wout_ref = bf16[1152,1152]{1,0:T(8,128)(2,1)} reshape(bf16[32,36,1152]{2,1,0:T(8,128)(2,1)} %all-gather.7.cloned.1.call-done) | data formatting | bytes 5308416
  89.5 63.2 %all-gather.5.cloned.1.call-done = bf16[32,108,1152]{2,1,0:T(8,128)(2,1)} async-done(((bf16[1,108,1152]{2,1,0:T(8,128)(2,1)}), bf16[32,108,1152]{2,1,0:T(8,128)(2,1)}) %all-gather.5.cloned.1.call-update) | async-done | bytes 7962640 | tf_op jit(solution)/shard_map/all_gather | solution.py:152
  152.6 9.2 %reshape.2.wqkv_ref = bf16[3456,1152]{1,0:T(8,128)(2,1)} reshape(bf16[32,108,1152]{2,1,0:T(8,128)(2,1)} %all-gather.5.cloned.1.call-done) | data formatting | bytes 15925248
  161.9 55.5 %shard_map.55 = bf16[20,64,1152]{2,1,0:T(8,128)(2,1)} custom-call(s32[1]{0:T(128)S(6)} %copy.18.len_ref, bf16[20,64,1152]{2,1,0:T(8,128)(2,1)} %bitcast.22, f32[3,1152]{1,0:T(4,128)} %bitcast.25, bf16[3456,1152]{1,0:T(8,128)(2,1)} %reshape.2.wqkv_ref, bf16[1152,1152]{1,0:T(8,128)(2,1)} %reshape.4.wout_ref), custom_call_target="tpu_custom_call" | custom-call | tf_op jit(solution)/shard_map/pallas_call | solution.py:158
  217.4 38.0 %all_to_all.33 = bf16[20,64,1152]{2,1,0:T(8,128)(2,1)S(1)} all-to-all(bf16[20,64,1152]{2,1,0:T(8,128)(2,1)} %shard_map.55), channel_id=1, replica_groups=mesh['clip'=8,'grp'=4] {'grp'}, dimensions={0} | all-to-all | bytes 5898240 | tf_op jit(solution)/shard_map/all_to_all | solution.py:172
  255.4 1.9 copy.12
Async XLA Ops:
  6.5 77.8 %all-gather.7.cloned.1.call-start = ((), (), s32[]{:S(2)}) async-start(), calls=%async_computation.3 | async-start | bytes 3041280 | tf_op jit(solution)/shard_map/all_gather | solution.py:153
  7.3 145.4 %all-gather.5.cloned.1.call-start = ((), (), s32[]{:S(2)}) async-start(), calls=%async_computation.2 | async-start | bytes 8515584 | tf_op jit(solution)/shard_map/all_gather | solution.py:152
  13.8 5.7 %copy-start = (f32[1,3,1152]{2,0,1:T(1,128)S(1)}, f32[1,3,1152]{2,0,1:T(1,128)}, u32[]{:S(2)}) copy-start(f32[1,3,1152]{2,0,1:T(1,128)} %param.6) | copy-start | bytes 41476
  13.8 66.1 %all-to-all-start = ((bf16[5,256,1152]{2,0,1:T(8,128)(2,1)}), bf16[5,256,1152]{2,0,1:T(8,128)(2,1)}, u32[]{:S(2)}, u32[]{:S(2)}) async-start(bf16[5,256,1152]{2,0,1:T(8,128)(2,1)} %bitcast.20), calls=%async_computation | async-start | bytes 9437184 | tf_op jit(solution)/shard_map/all_to_all | solution.py:154
Sparse Core Ops, SparseCore 0:
  10.2 64.1 all-gather.6
  77.3 75.3 all-gather.4

commit v2 on v1

--- a/solution.py
+++ b/solution.py
@@ -122,54 +122,330 @@
     lax.fori_loop(0, frames, close, 0)
 
 
-def kernel(len_ref, x_ref, table_ref, wqkv_ref, wout_ref, out_ref, mod_ref, qkv_ref, bias_ref, mixed_ref, proj_ref):
-    frames, tokens, width = x_ref.shape
+def ceil16(n):
+    return (n + 15) // 16 * 16
+
+
+def kernel(
+    sizes, len_ref, hid_ref, table_ref, shard_ref, out_ref,
+    x_ref, w_ref, stage_ref, wqkv_ref, wout_ref, mod_ref, qkv_ref, bias_ref, mixed_ref, proj_ref, done_ref,
+    local_sem, y_send, y_recv, right_send, right_recv, left_send, left_recv, x_send, x_recv, k_send, k_recv,
+    in_send, in_recv, back_send, back_recv, back_local,
+):
+    zs, ys, group, shard_rows, qkv_rows, out_rows, clips_step = sizes
+    own, all_tokens, width = hid_ref.shape
+    frames, tokens, _ = x_ref.shape
+    blocks = tokens // PAIR
+    clip, grp = lax.axis_index("clip"), lax.axis_index("grp")
+    z, x = clip // 2, clip % 2
+    y, k = grp // 2, grp % 2
+    mesh_ids = pl.DeviceIdType.MESH
     length = len_ref[0]
+
+    def mate(step):
+        return lax.rem(grp + step, group)
+
+    def at(z_to, x_to):
+        return (z_to * 2 + x_to, grp)
+
+    barrier = pltpu.get_barrier_semaphore()
+    for step in range(1, group):
+        pl.semaphore_signal(barrier, inc=1, device_id=(clip, mate(step)), device_id_type=mesh_ids)
+    pl.semaphore_signal(barrier, inc=1, device_id=at(z, 1 - x), device_id_type=mesh_ids)
+
+    @pl.when(z > 0)
+    def _():
+        pl.semaphore_signal(barrier, inc=1, device_id=at(z - 1, x), device_id_type=mesh_ids)
+
+    @pl.when(z < zs - 1)
+    def _():
+        pl.semaphore_signal(barrier, inc=1, device_id=at(z + 1, x), device_id_type=mesh_ids)
+
+    own_w = pltpu.make_async_copy(
+        shard_ref, w_ref.at[z, x, k, pl.ds(pl.multiple_of(y * shard_rows, 16), shard_rows)], local_sem.at[0]
+    )
+    own_w.start()
+    own_x = pltpu.make_async_copy(
+        hid_ref.at[:, pl.ds(pl.multiple_of(grp * tokens, PAIR), tokens)],
+        x_ref.at[pl.ds(grp * own, own)], local_sem.at[1],
+    )
+    own_x.start()
+    ends = jnp.where(z > 0, 1, 0) + jnp.where(z < zs - 1, 1, 0)
+    pl.semaphore_wait(barrier, group + ends)
+
+    def remote(src, dst, send, recv, to):
+        return pltpu.make_async_remote_copy(
+            src_ref=src, dst_ref=dst, send_sem=send, recv_sem=recv, device_id=to, device_id_type=mesh_ids
+        )
+
+    def y_copy(step):
+        rows = pl.ds(pl.multiple_of(y * shard_rows, 16), shard_rows)
+        to = (clip, lax.rem(y + step, ys) * 2 + k)
+        return remote(shard_ref, w_ref.at[z, x, k, rows], y_send.at[step], y_recv.at[step], to)
+
+    def in_copy(step):
+        to = mate(step)
+        src = hid_ref.at[:, pl.ds(pl.multiple_of(to * tokens, PAIR), tokens)]
+        return remote(src, x_ref.at[pl.ds(grp * own, own)], in_send.at[step], in_recv.at[step], (clip, to))
+
+    def right_copy(origin, hop):
+        slot = w_ref.at[origin, x, k]
+        return remote(slot, slot, right_send.at[hop], right_recv.at[hop], at(z + 1, x))
+
+    def left_copy(origin, hop):
+        slot = w_ref.at[origin, x, k]
+        return remote(slot, slot, left_send.at[hop], left_recv.at[hop], at(z - 1, x))
+
+    def x_copy(origin):
+        slot = w_ref.at[origin, x, k]
+        return remote(slot, slot, x_send.at[origin], x_recv.at[origin], at(z, 1 - x))
+
+    def k_copy(origin, x_of):
+        slot = w_ref.at[origin, x_of, k]
+        return remote(slot, slot, k_send.at[x_of, origin], k_recv.at[x_of, origin], (clip, y * 2 + 1 - k))
+
+    for step in range(1, ys):
+        y_copy(step).start()
+    own_w.wait()
+    for step in range(1, group):
+        in_copy(step).start()
     make_bias(bias_ref, length)
-
-    def first(step, carry):
-        modulate_step(step, x_ref, table_ref, mod_ref)
-        return carry
-
-    lax.fori_loop(0, frames // 2 * (tokens // PAIR), first, 0)
+    for step in range(1, ys):
+        y_copy(step).wait_recv()
+
+    x_copy(z).start()
+
+    @pl.when(z < zs - 1)
+    def _():
+        right_copy(z, 0).start()
+
+    @pl.when(z > 0)
+    def _():
+        left_copy(z, 0).start()
+
+    k_copy(z, x).start()
+
+    def pass_on(hop):
+        @pl.when(z - hop >= 0)
+        def _():
+            right_copy(z - hop, hop - 1).wait_recv()
+
+            @pl.when(z < zs - 1)
+            def _():
+                right_copy(z - hop, hop).start()
+
+            x_copy(z - hop).start()
+            k_copy(z - hop, x).start()
+
+        @pl.when(z + hop < zs)
+        def _():
+            left_copy(z + hop, hop - 1).wait_recv()
+
+            @pl.when(z > 0)
+            def _():
+                left_copy(z + hop, hop).start()
+
+            x_copy(z + hop).start()
+            k_copy(z + hop, x).start()
+
+    def share(hop):
+        def one(origin):
+            x_copy(origin).wait_recv()
+            k_copy(origin, 1 - x).start()
+
+        if hop == 0:
+            one(z)
+            return
+
+        @pl.when(z - hop >= 0)
+        def _():
+            one(z - hop)
+
+        @pl.when(z + hop < zs)
+        def _():
+            one(z + hop)
+
+    near = z < zs // 2
+    groups = zs * 2 // clips_step
     rows = 2 * frames * HALF
-
-    def second(step, carry):
-        qkv_step(step, mod_ref, wqkv_ref, qkv_ref, rows)
-        return carry
-
-    lax.fori_loop(0, (mod_ref.shape[0] // rows) * (3 * width // col_tile(3 * width)), second, 0)
+    tile = col_tile(3 * width)
+    tiles = 3 * width // tile
+    parts = mod_ref.shape[0] // rows
+    span_qkv = clips_step * group * qkv_rows
+    span_out = clips_step * group * out_rows
+
+    def take(origin):
+        for x_of in range(2):
+            k_copy(origin, x_of).wait_recv()
+
+    def gather_group(index):
+        for c in range(clips_step):
+            clip_of = index * clips_step + c
+            for g in range(group):
+                slot = w_ref.at[clip_of // 2, clip_of % 2, g % 2]
+                base = (g // 2) * shard_rows
+                n = c * group + g
+                stage_ref[n * qkv_rows : (n + 1) * qkv_rows, :] = slot[base : base + qkv_rows, :]
+                stage_ref[span_qkv + n * out_rows : span_qkv + (n + 1) * out_rows, :] = slot[
+                    base + qkv_rows : base + qkv_rows + out_rows, :
+                ]
+        wqkv_ref[pl.ds(pl.multiple_of(index * span_qkv, 16), span_qkv), :] = stage_ref[0:span_qkv, :]
+        wout_ref[pl.ds(pl.multiple_of(index * span_out, 16), span_out), :] = stage_ref[
+            span_qkv : span_qkv + span_out, :
+        ]
+
+    def columns(count_from, count_to):
+        def one(step, carry):
+            place = step // parts
+            place = jnp.where(near, place, tiles - 1 - place)
+            m = pl.multiple_of(lax.rem(step, parts) * rows, 16)
+            n = pl.multiple_of(place * tile, 128)
+            got = lax.dot_general(
+                mod_ref[pl.ds(m, rows), :], wqkv_ref[pl.ds(n, tile), :], NT,
+                preferred_element_type=jnp.float32,
+            )
+            qkv_ref[pl.ds(m, rows), pl.ds(n, tile)] = got.astype(jnp.bfloat16)
+            return carry
+
+        lax.fori_loop(count_from * parts, count_to * parts, one, 0)
+
+    def advance(first, last, tile_from, tile_to):
+        for ordinal in range(first, last):
+            take(jnp.where(near, ordinal, zs - 1 - ordinal))
+        begin, end = first * groups // zs, last * groups // zs
+
+        def one(step, carry):
+            gather_group(jnp.where(near, step, groups - 1 - step))
+            return carry
+
+        lax.fori_loop(begin, end, one, 0)
+        columns(tile_from, tile_to)
+
+    def modulate_all():
+        own_x.wait()
+        for step in range(1, group):
+            in_copy(step).wait_recv()
+
+        def first(step, carry):
+            modulate_step(step, x_ref, table_ref, mod_ref)
+            return carry
+
+        lax.fori_loop(0, frames // 2 * blocks, first, 0)
+
+    def ready(ordinals):
+        return min(ordinals * groups // zs * span_qkv // tile, tiles)
+
+    for hop in range(1, zs):
+        pass_on(hop)
+        share(hop - 1)
+        if hop == zs // 2:
+            modulate_all()
+            advance(0, 1, 0, ready(1))
+        if hop > zs // 2:
+            advance(hop - zs // 2, hop - zs // 2 + 1, ready(hop - zs // 2), ready(hop - zs // 2 + 1))
+    share(zs - 1)
+    left = zs // 2
+    for ordinal in range(left, zs):
+        advance(ordinal, ordinal + 1, ready(ordinal), ready(ordinal + 1))
+
+    def back_copy(step, block):
+        to = mate(step)
+        src = done_ref.at[pl.ds(to * own, own), pl.ds(pl.multiple_of(block * PAIR, PAIR), PAIR)]
+        dst = out_ref.at[:, pl.ds(pl.multiple_of(grp * tokens + block * PAIR, PAIR), PAIR)]
+        return remote(src, dst, back_send.at[step, block], back_recv.at[step, block], (clip, to))
+
+    def back_own(block):
+        src = done_ref.at[pl.ds(grp * own, own), pl.ds(pl.multiple_of(block * PAIR, PAIR), PAIR)]
+        dst = out_ref.at[:, pl.ds(pl.multiple_of(grp * tokens + block * PAIR, PAIR), PAIR)]
+        return pltpu.make_async_copy(src, dst, back_local.at[block])
 
     def third(block, carry):
-        finish_block(block, x_ref, table_ref, length, qkv_ref, bias_ref, mixed_ref, proj_ref, wout_ref, out_ref)
-        return carry
-
-    lax.fori_loop(0, tokens // PAIR, third, 0)
+        finish_block(block, x_ref, table_ref, length, qkv_ref, bias_ref, mixed_ref, proj_ref, wout_ref, done_ref)
+        for step in range(1, group):
+            back_copy(step, block).start()
+        back_own(block).start()
+        return carry
+
+    lax.fori_loop(0, blocks, third, 0)
+
+    for step in range(1, ys):
+        y_copy(step).wait_send()
+    for step in range(1, group):
+        in_copy(step).wait_send()
+    for hop in range(zs - 1):
+
+        @pl.when((z - hop >= 0) & (z < zs - 1))
+        def _():
+            right_copy(z - hop, hop).wait_send()
+
+        @pl.when((z + hop < zs) & (z > 0))
+        def _():
+            left_copy(z + hop, hop).wait_send()
+
+    def sent(origin, carry):
+        x_copy(origin).wait_send()
+        for x_of in range(2):
+            k_copy(origin, x_of).wait_send()
+        return carry
+
+    lax.fori_loop(0, zs, sent, 0)
+
+    def returned(block, carry):
+        for step in range(1, group):
+            back_copy(step, block).wait_send()
+            back_copy(step, block).wait_recv()
+        back_own(block).wait()
+        return carry
+
+    lax.fori_loop(0, blocks, returned, 0)
 
 
 def on_device(hidden, modulation, clip_frames, qkv_weight, out_weight):
-    both = ("clip", "grp")
-    wqkv = lax.all_gather(qkv_weight.T, both, axis=0, tiled=True)
-    wout = lax.all_gather(out_weight.T, both, axis=0, tiled=True)
-    x = lax.all_to_all(hidden[0], "grp", split_axis=1, concat_axis=0, tiled=True)
-    frames, tokens, width = x.shape
+    clips, group = lax.axis_size("clip"), lax.axis_size("grp")
+    zs, ys = clips // 2, group // 2
+    _, own, all_tokens, width = hidden.shape
+    frames, tokens = own * group, all_tokens // group
+    qkv_rows, out_rows = qkv_weight.shape[1], out_weight.shape[1]
+    shard_rows = ceil16(qkv_rows + out_rows)
+    clips_step = 1
+    while clips_step * group * qkv_rows % 16 or clips_step * group * out_rows % 16:
+        clips_step *= 2
+    spare = jnp.zeros((shard_rows - qkv_rows - out_rows, width), jnp.bfloat16)
+    shard = jnp.concatenate([qkv_weight.T, out_weight.T, spare], axis=0)
     rows = frames * HALF
+    blocks = tokens // PAIR
     vmem = pl.BlockSpec(memory_space=pltpu.VMEM)
+    hbm = pl.BlockSpec(memory_space=pl.ANY)
+    dma = pltpu.SemaphoreType.DMA
+    bf16 = jnp.bfloat16
+    sizes = (zs, ys, group, shard_rows, qkv_rows, out_rows, clips_step)
     out = pl.pallas_call(
-        kernel,
-        out_shape=jax.ShapeDtypeStruct(x.shape, jnp.bfloat16),
-        in_specs=[pl.BlockSpec(memory_space=pltpu.SMEM)] + [vmem] * 4,
-        out_specs=vmem,
+        functools.partial(kernel, sizes),
+        out_shape=jax.ShapeDtypeStruct((own, all_tokens, width), bf16),
+        in_specs=[pl.BlockSpec(memory_space=pltpu.SMEM), hbm, vmem, hbm],
+        out_specs=hbm,
         scratch_shapes=[
-            pltpu.VMEM((frames * tokens, width), jnp.bfloat16),
-            pltpu.VMEM((frames * tokens, 3 * width), jnp.bfloat16),
+            pltpu.VMEM((frames, tokens, width), bf16),
+            pltpu.VMEM((zs, 2, 2, ys * shard_rows, width), bf16),
+            pltpu.VMEM((clips_step * group * (qkv_rows + out_rows), width), bf16),
+            pltpu.VMEM((3 * width, width), bf16),
+            pltpu.VMEM((width, width), bf16),
+            pltpu.VMEM((frames * tokens, width), bf16),
+            pltpu.VMEM((frames * tokens, 3 * width), bf16),
             pltpu.VMEM((rows, rows), jnp.float32),
-            pltpu.VMEM((2 * rows, width), jnp.bfloat16),
+            pltpu.VMEM((2 * rows, width), bf16),
             pltpu.VMEM((2 * rows, width), jnp.float32),
+            pltpu.VMEM((frames, tokens, width), bf16),
+            dma((2,)), dma((ys,)), dma((ys,)),
+            dma((zs,)), dma((zs,)), dma((zs,)), dma((zs,)),
+            dma((zs,)), dma((zs,)), dma((2, zs)), dma((2, zs)),
+            dma((group,)), dma((group,)), dma((group, blocks)), dma((group, blocks)), dma((blocks,)),
         ],
-        compiler_params=pltpu.CompilerParams(vmem_limit_bytes=56 * 1024 * 1024),
-    )(clip_frames, x, modulation[0], wqkv, wout)
-    return lax.all_to_all(out, "grp", split_axis=0, concat_axis=1, tiled=True)[None]
+        compiler_params=pltpu.CompilerParams(
+            collective_id=0, has_side_effects=True, vmem_limit_bytes=58 * 1024 * 1024
+        ),
+    )(clip_frames, hidden[0], modulation[0], shard)
+    return out[None]
 
 
 def solution(mesh):

time: 267 us -> 133 us (0.50); the launches traced: 264 us -> 133 us
  waiting for transfers between devices: 124 us -> 0 us
  Pallas kernels: 55.5 us -> 126 us
  blocking collectives: 38 us -> 0 us
  local copies, waits for them, and re-layouts: 27.1 us -> 4.97 us
  between operations: 14.1 us -> 0.66 us
  starting transfers between devices: 5.74 us -> 0 us
    pallas_call x1, Pallas kernels: 55.5 us -> 126 us  [on_device(): pl.pallas_call(functools.partial(kernel, sizes), out_shape=jax.ShapeDtype...]
    all_gather x2 -> x0, waiting for transfers between devices: 63.2 us -> none  [the longest x1 63.2 us: on_device(): wqkv = lax.all_gather(qkv_weight.T, both, axis=0, tiled=True)]
    all_to_all x1 -> x0, waiting for transfers between devices: 59.1 us -> none  [on_device(): lax.all_to_all(hidden[0], 'grp', split_axis=1, concat_axis=0, tiled=True)]
    all_to_all x1 -> x0, blocking collectives: 38 us -> none  [on_device(): lax.all_to_all(out, 'grp', split_axis=0, concat_axis=1, tiled=True)[None]]
    unnamed x6 -> x2, local copies, waits for them, and re-layouts: 20.8 us -> 4.97 us
    all_to_all x2 -> x0, local copies, waits for them, and re-layouts: 6.36 us -> none  [the longest x1 4.48 us: on_device(): lax.all_to_all(hidden[0], 'grp', split_axis=1, concat_axis=0, tiled=True)]
    all_to_all x1 -> x0, starting transfers between devices: 5.7 us -> none  [on_device(): lax.all_to_all(hidden[0], 'grp', split_axis=1, concat_axis=0, tiled=True)]
  transfers between devices with their start and end apart: 3 -> 0, of which waited for: 2 -> 0; matrix products, arithmetic and copies ran while one was open for 6% -> 0% of each run, Pallas kernels for 0% -> 0%
where the time goes in v2:
time: 133 us
  Pallas kernels  126 us (95%)
  local copies, waits for them, and re-layouts  4.97 us (4%)
  other arithmetic  1.75 us (1%)
    pallas_call x1, Pallas kernels, on_device(): pl.pallas_call(functools.partial(kernel, sizes), out_shape=jax.ShapeDtype...  126 us
    unnamed x2, local copies, waits for them, and re-layouts  4.97 us

profile of v2, /device:TPU:17, one launch (start us, length us, event | category | flops | bytes accessed | tf_op | source)
XLA Modules:
  0.0 133.0 jit_solution(2796794019133231628)
XLA Ops:
  0.7 1.3 copy.8
  2.0 1.8 %pad_maximum_fusion.shard_ref = bf16[144,1152]{1,0:T(8,128)(2,1)} fusion(bf16[36,1152]{1,0:T(8,128)(2,1)} %bitcast.10, bf16[108,1152]{1,0:T(8,128)(2,1)} %bitcast.9), kind=kLoop, calls=%fused_computation | loop fusion | flops 663552 | bytes 663552 | tf_op jit(solution)/shard_map/concatenate | solution.py:414
  3.7 125.6 %shard_map.55 = bf16[5,256,1152]{2,1,0:T(8,128)(2,1)} custom-call(s32[1]{0:T(128)S(6)} %copy.10.len_ref, bf16[5,256,1152]{2,1,0:T(8,128)(2,1)} %bitcast.8, f32[3,1152]{1,0:T(4,128)} %bitcast.11, bf16[144,1152]{1,0:T(8,128)(2,1)} %pad_maximum_fusion.shard_ref), custom_call_target="tpu_custom_call" | custom-call | tf_op jit(solution)/shard_map/pallas_call | solution.py:422
  129.3 3.7 %copy.11 = bf16[1,5,256,1152]{3,2,1,0:T(8,128)(2,1)} copy(bf16[1,5,256,1152]{3,2,1,0:T(8,128)(2,1)} %bitcast.7) | data formatting | bytes 5898240

commit v3 on v2

--- a/solution.py
+++ b/solution.py
@@ -60,6 +60,7 @@
     head = width // HEADS
     scale = head**-0.5 * LOG2E
     tiles = [None] * (width // 128)
+    ones = jnp.ones((rows, 128), jnp.bfloat16)
     for h in range(HEADS):
         low, high = h * head, (h + 1) * head
         w0 = low // 128 * 128
@@ -73,11 +74,12 @@
         s = lax.dot_general(q, k, NT, preferred_element_type=jnp.float32)
         s = s * scale + bias_ref[...]
         p = jnp.exp2(s - jnp.max(s, axis=-1, keepdims=True))
-        total = jnp.sum(p, axis=-1, keepdims=True)
-        o = jnp.dot(p.astype(jnp.bfloat16), v, preferred_element_type=jnp.float32)
-        o = o * (1.0 / total)
+        p = p.astype(jnp.bfloat16)
+        total = jnp.dot(p, ones, preferred_element_type=jnp.float32)
+        share = 1.0 / total
+        o = jnp.dot(p, v, preferred_element_type=jnp.float32)
         for t in range(w0 // 128, w1 // 128):
-            part = o[:, t * 128 - w0 : t * 128 - w0 + 128]
+            part = o[:, t * 128 - w0 : t * 128 - w0 + 128] * share
             where = inside[:, t * 128 - w0 : t * 128 - w0 + 128]
             tiles[t] = part if tiles[t] is None else jnp.where(where, part, tiles[t])
             if high >= (t + 1) * 128:
@@ -127,7 +129,7 @@
 
 
 def kernel(
-    sizes, len_ref, hid_ref, table_ref, shard_ref, out_ref,
+    sizes, len_ref, hid_ref, table_ref, own_qkv_ref, own_out_ref, out_ref,
     x_ref, w_ref, stage_ref, wqkv_ref, wout_ref, mod_ref, qkv_ref, bias_ref, mixed_ref, proj_ref, done_ref,
     local_sem, y_send, y_recv, right_send, right_recv, left_send, left_recv, x_send, x_recv, k_send, k_recv,
     in_send, in_recv, back_send, back_recv, back_local,
@@ -161,13 +163,12 @@
     def _():
         pl.semaphore_signal(barrier, inc=1, device_id=at(z + 1, x), device_id_type=mesh_ids)
 
-    own_w = pltpu.make_async_copy(
-        shard_ref, w_ref.at[z, x, k, pl.ds(pl.multiple_of(y * shard_rows, 16), shard_rows)], local_sem.at[0]
-    )
-    own_w.start()
+    stage_ref[0:qkv_rows, :] = own_qkv_ref[...]
+    stage_ref[qkv_rows : qkv_rows + out_rows, :] = own_out_ref[...]
+    w_ref[z, x, k, pl.ds(pl.multiple_of(y * shard_rows, 16), shard_rows), :] = stage_ref[0:shard_rows, :]
     own_x = pltpu.make_async_copy(
         hid_ref.at[:, pl.ds(pl.multiple_of(grp * tokens, PAIR), tokens)],
-        x_ref.at[pl.ds(grp * own, own)], local_sem.at[1],
+        x_ref.at[pl.ds(grp * own, own)], local_sem.at[0],
     )
     own_x.start()
     ends = jnp.where(z > 0, 1, 0) + jnp.where(z < zs - 1, 1, 0)
@@ -178,92 +179,103 @@
             src_ref=src, dst_ref=dst, send_sem=send, recv_sem=recv, device_id=to, device_id_type=mesh_ids
         )
 
+    def slot_of(origin, x_of, dy):
+        rows = pl.multiple_of(lax.rem(y + dy, ys) * shard_rows, 16)
+        return w_ref.at[origin, x_of, k, pl.ds(rows, shard_rows)]
+
     def y_copy(step):
-        rows = pl.ds(pl.multiple_of(y * shard_rows, 16), shard_rows)
         to = (clip, lax.rem(y + step, ys) * 2 + k)
-        return remote(shard_ref, w_ref.at[z, x, k, rows], y_send.at[step], y_recv.at[step], to)
+        slot = slot_of(z, x, 0)
+        return remote(slot, slot, y_send.at[step], y_recv.at[step], to)
 
     def in_copy(step):
         to = mate(step)
         src = hid_ref.at[:, pl.ds(pl.multiple_of(to * tokens, PAIR), tokens)]
         return remote(src, x_ref.at[pl.ds(grp * own, own)], in_send.at[step], in_recv.at[step], (clip, to))
 
-    def right_copy(origin, hop):
-        slot = w_ref.at[origin, x, k]
-        return remote(slot, slot, right_send.at[hop], right_recv.at[hop], at(z + 1, x))
-
-    def left_copy(origin, hop):
-        slot = w_ref.at[origin, x, k]
-        return remote(slot, slot, left_send.at[hop], left_recv.at[hop], at(z - 1, x))
-
-    def x_copy(origin):
-        slot = w_ref.at[origin, x, k]
-        return remote(slot, slot, x_send.at[origin], x_recv.at[origin], at(z, 1 - x))
-
-    def k_copy(origin, x_of):
-        slot = w_ref.at[origin, x_of, k]
-        return remote(slot, slot, k_send.at[x_of, origin], k_recv.at[x_of, origin], (clip, y * 2 + 1 - k))
+    def right_copy(origin, hop, dy):
+        slot = slot_of(origin, x, dy)
+        return remote(slot, slot, right_send.at[hop, dy], right_recv.at[hop, dy], at(z + 1, x))
+
+    def left_copy(origin, hop, dy):
+        slot = slot_of(origin, x, dy)
+        return remote(slot, slot, left_send.at[hop, dy], left_recv.at[hop, dy], at(z - 1, x))
+
+    def x_copy(origin, dy):
+        slot = slot_of(origin, x, dy)
+        return remote(slot, slot, x_send.at[origin, dy], x_recv.at[origin, dy], at(z, 1 - x))
+
+    def k_copy(origin, x_of, dy):
+        slot = slot_of(origin, x_of, dy)
+        to = (clip, y * 2 + 1 - k)
+        return remote(slot, slot, k_send.at[x_of, origin, dy], k_recv.at[x_of, origin, dy], to)
+
+    def begin(dy):
+        x_copy(z, dy).start()
+
+        @pl.when(z < zs - 1)
+        def _():
+            right_copy(z, 0, dy).start()
+
+        @pl.when(z > 0)
+        def _():
+            left_copy(z, 0, dy).start()
+
+        k_copy(z, x, dy).start()
 
     for step in range(1, ys):
         y_copy(step).start()
-    own_w.wait()
-    for step in range(1, group):
-        in_copy(step).start()
+    begin(0)
     make_bias(bias_ref, length)
     for step in range(1, ys):
         y_copy(step).wait_recv()
-
-    x_copy(z).start()
-
-    @pl.when(z < zs - 1)
-    def _():
-        right_copy(z, 0).start()
-
-    @pl.when(z > 0)
-    def _():
-        left_copy(z, 0).start()
-
-    k_copy(z, x).start()
+        begin(ys - step)
+    for step in range(1, group):
+        in_copy(step).start()
 
     def pass_on(hop):
-        @pl.when(z - hop >= 0)
-        def _():
-            right_copy(z - hop, hop - 1).wait_recv()
-
-            @pl.when(z < zs - 1)
+        for dy in range(ys):
+
+            @pl.when(z - hop >= 0)
             def _():
-                right_copy(z - hop, hop).start()
-
-            x_copy(z - hop).start()
-            k_copy(z - hop, x).start()
-
-        @pl.when(z + hop < zs)
-        def _():
-            left_copy(z + hop, hop - 1).wait_recv()
-
-            @pl.when(z > 0)
+                right_copy(z - hop, hop - 1, dy).wait_recv()
+                x_copy(z - hop, dy).start()
+
+                @pl.when(z < zs - 1)
+                def _():
+                    right_copy(z - hop, hop, dy).start()
+
+                k_copy(z - hop, x, dy).start()
+
+            @pl.when(z + hop < zs)
             def _():
-                left_copy(z + hop, hop).start()
-
-            x_copy(z + hop).start()
-            k_copy(z + hop, x).start()
+                left_copy(z + hop, hop - 1, dy).wait_recv()
+                x_copy(z + hop, dy).start()
+
+                @pl.when(z > 0)
+                def _():
+                    left_copy(z + hop, hop, dy).start()
+
+                k_copy(z + hop, x, dy).start()
 
     def share(hop):
-        def one(origin):
-            x_copy(origin).wait_recv()
-            k_copy(origin, 1 - x).start()
-
-        if hop == 0:
-            one(z)
-            return
-
-        @pl.when(z - hop >= 0)
-        def _():
-            one(z - hop)
-
-        @pl.when(z + hop < zs)
-        def _():
-            one(z + hop)
+        for dy in range(ys):
+
+            def one(origin):
+                x_copy(origin, dy).wait_recv()
+                k_copy(origin, 1 - x, dy).start()
+
+            if hop == 0:
+                one(z)
+                continue
+
+            @pl.when(z - hop >= 0)
+            def _():
+                one(z - hop)
+
+            @pl.when(z + hop < zs)
+            def _():
+                one(z + hop)
 
     near = z < zs // 2
     groups = zs * 2 // clips_step
@@ -276,7 +288,8 @@
 
     def take(origin):
         for x_of in range(2):
-            k_copy(origin, x_of).wait_recv()
+            for dy in range(ys):
+                k_copy(origin, x_of, dy).wait_recv()
 
     def gather_group(index):
         for c in range(clips_step):
@@ -338,14 +351,10 @@
     for hop in range(1, zs):
         pass_on(hop)
         share(hop - 1)
-        if hop == zs // 2:
-            modulate_all()
-            advance(0, 1, 0, ready(1))
-        if hop > zs // 2:
-            advance(hop - zs // 2, hop - zs // 2 + 1, ready(hop - zs // 2), ready(hop - zs // 2 + 1))
-    share(zs - 1)
-    left = zs // 2
-    for ordinal in range(left, zs):
+    modulate_all()
+    for ordinal in range(zs):
+        if ordinal == zs - 1:
+            share(zs - 1)
         advance(ordinal, ordinal + 1, ready(ordinal), ready(ordinal + 1))
 
     def back_copy(step, block):
@@ -376,16 +385,19 @@
 
         @pl.when((z - hop >= 0) & (z < zs - 1))
         def _():
-            right_copy(z - hop, hop).wait_send()
+            for dy in range(ys):
+                right_copy(z - hop, hop, dy).wait_send()
 
         @pl.when((z + hop < zs) & (z > 0))
         def _():
-            left_copy(z + hop, hop).wait_send()
+            for dy in range(ys):
+                left_copy(z + hop, hop, dy).wait_send()
 
     def sent(origin, carry):
-        x_copy(origin).wait_send()
-        for x_of in range(2):
-            k_copy(origin, x_of).wait_send()
+        for dy in range(ys):
+            x_copy(origin, dy).wait_send()
+            for x_of in range(2):
+                k_copy(origin, x_of, dy).wait_send()
         return carry
 
     lax.fori_loop(0, zs, sent, 0)
@@ -410,8 +422,6 @@
     clips_step = 1
     while clips_step * group * qkv_rows % 16 or clips_step * group * out_rows % 16:
         clips_step *= 2
-    spare = jnp.zeros((shard_rows - qkv_rows - out_rows, width), jnp.bfloat16)
-    shard = jnp.concatenate([qkv_weight.T, out_weight.T, spare], axis=0)
     rows = frames * HALF
     blocks = tokens // PAIR
     vmem = pl.BlockSpec(memory_space=pltpu.VMEM)
@@ -422,7 +432,7 @@
     out = pl.pallas_call(
         functools.partial(kernel, sizes),
         out_shape=jax.ShapeDtypeStruct((own, all_tokens, width), bf16),
-        in_specs=[pl.BlockSpec(memory_space=pltpu.SMEM), hbm, vmem, hbm],
+        in_specs=[pl.BlockSpec(memory_space=pltpu.SMEM), hbm, vmem, vmem, vmem],
         out_specs=hbm,
         scratch_shapes=[
             pltpu.VMEM((frames, tokens, width), bf16),
@@ -436,15 +446,15 @@
             pltpu.VMEM((2 * rows, width), bf16),
             pltpu.VMEM((2 * rows, width), jnp.float32),
             pltpu.VMEM((frames, tokens, width), bf16),
-            dma((2,)), dma((ys,)), dma((ys,)),
-            dma((zs,)), dma((zs,)), dma((zs,)), dma((zs,)),
-            dma((zs,)), dma((zs,)), dma((2, zs)), dma((2, zs)),
+            dma((1,)), dma((ys,)), dma((ys,)),
+            dma((zs, ys)), dma((zs, ys)), dma((zs, ys)), dma((zs, ys)),
+            dma((zs, ys)), dma((zs, ys)), dma((2, zs, ys)), dma((2, zs, ys)),
             dma((group,)), dma((group,)), dma((group, blocks)), dma((group, blocks)), dma((blocks,)),
         ],
         compiler_params=pltpu.CompilerParams(
             collective_id=0, has_side_effects=True, vmem_limit_bytes=58 * 1024 * 1024
         ),
-    )(clip_frames, hidden[0], modulation[0], shard)
+    )(clip_frames, hidden[0], modulation[0], qkv_weight.T, out_weight.T)
     return out[None]
 
 

time: 133 us -> 152 us (1.14)
  Pallas kernels: 126 us -> 147 us
  other arithmetic: 1.75 us -> 0 us
    pallas_call x1, Pallas kernels: 126 us -> 147 us  [on_device(): pl.pallas_call(functools.partial(kernel, sizes), out_shape=jax.ShapeDtype...]
    concatenate x1 -> x0, other arithmetic: 1.75 us -> none  [on_device(): shard = jnp.concatenate([qkv_weight.T, out_weight.T, spare], axis=0)]
where the time goes in v3:
time: 152 us
  Pallas kernels  147 us (97%)
  local copies, waits for them, and re-layouts  4.98 us (3%)
    pallas_call x1, Pallas kernels, on_device(): pl.pallas_call(functools.partial(kernel, sizes), out_shape=jax.ShapeDtype...  147 us
    unnamed x2, local copies, waits for them, and re-layouts  4.98 us

profile of v3, /device:TPU:17, one launch (start us, length us, event | category | flops | bytes accessed | tf_op | source)
XLA Modules:
  0.0 152.2 jit_solution(11853124454680114785)
XLA Ops:
  0.7 1.3 copy.8
  2.0 146.5 %shard_map.55 = bf16[5,256,1152]{2,1,0:T(8,128)(2,1)} custom-call(s32[1]{0:T(128)S(6)} %copy.10.len_ref, bf16[5,256,1152]{2,1,0:T(8,128)(2,1)} %bitcast.8, f32[3,1152]{1,0:T(4,128)} %bitcast.11, bf16[108,1152]{1,0:T(8,128)(2,1)} %bitcast.9, bf16[36,1152]{1,0:T(8,128)(2,1)} %bitcast.10), custom_call_target="tpu_custom_call" | custom-call | tf_op jit(solution)/shard_map/pallas_call | solution.py:432
  148.5 3.7 %copy.11 = bf16[1,5,256,1152]{3,2,1,0:T(8,128)(2,1)} copy(bf16[1,5,256,1152]{3,2,1,0:T(8,128)(2,1)} %bitcast.7) | data formatting | bytes 5898240
